TPU v7x, 256 devices: a whole 4x4x8 slice. The times are simulated.
256 devices in a mesh: store: 32 (over z, y), tp: 8 (over x, core).
Axes of the slice: x: 4, y: 4, z: 8, core: 2. Of those that a mesh axis runs over, the one named last changes fastest.
Arguments:
- query: bfloat16 [2560, 8192], P('store', 'tp')
- new_kv: bfloat16 [2, 2560, 1024], P(None, 'store', 'tp')
- kv_store: bfloat16 [2, 640, 512, 1024], P(None, 'store', None, 'tp'), may hold values from -6 to 6
- passage_ids: int32 [256, 10], P('store'), may hold values from 0 to 639, as said below
- residual_in: bfloat16 [2560, 8192], P('store', 'tp'), may hold values from -3 to 3
- out_weight: bfloat16 [8192, 8192], P('tp', 'store'), may hold values from -0.75 to 0.75
Outputs:
- layer_out: bfloat16 [2560, 8192], P('store', 'tp')
Inputs may be any that keep to these rules, and one draw needn't show every extreme that they name: `passage_ids`: store shard s holds passages s * 20 to (s + 1) * 20 - 1. In each aligned block of 8 rows (the queries of one index of store), every shard that is named at all is named exactly 5 times; popular shards are named in more blocks and low passage numbers within a shard are more popular.
All inputs are finite; a program needn't handle non-finite values.
Results may differ from a plain program's by a relative error of at most 0.018.
Values may be sent and summed in bfloat16 or wider, within the bound.
A program may use at most 64 MiB of HBM per device.

v0:
```python
import jax
import jax.numpy as jnp
from jax import lax
from jax.sharding import PartitionSpec as P

H = 64
KVH = 8
HD = 128
PLEN = 512


def attend_slots(queries, own_pairs, passage_local, kv_store):
    slot_count = queries.shape[0]
    kv_width = own_pairs.shape[1] // 2
    kv_heads = kv_width // HD
    group_size = H // KVH
    scaling = 1.0 / HD**0.5
    pass_local = kv_store.shape[1]
    query_heads = queries.reshape(slot_count, kv_heads, group_size, HD)
    own_keys = own_pairs[:, :kv_width].reshape(slot_count, kv_heads, HD)
    own_values = own_pairs[:, kv_width:].reshape(slot_count, kv_heads, HD)
    own_score = (
        jnp.einsum("bgjd,bgd->bgj", query_heads, own_keys, preferred_element_type=jnp.float32)
        * scaling
    )
    own_float = own_values.astype(jnp.float32)[:, :, None, :]

    def one_passage(index, result):
        block = lax.dynamic_index_in_dim(kv_store, index, 1, keepdims=False)
        stored_keys = block[0].reshape(PLEN, kv_heads, HD)
        stored_values = block[1].reshape(PLEN, kv_heads, HD)
        scores = (
            jnp.einsum(
                "bgjd,kgd->bgjk", query_heads, stored_keys, preferred_element_type=jnp.float32
            )
            * scaling
        )
        highest = jnp.maximum(jnp.max(scores, axis=-1), own_score)
        exponent_terms = jnp.exp(scores - highest[..., None])
        own_term = jnp.exp(own_score - highest)
        totals = jnp.sum(exponent_terms, axis=-1) + own_term
        weights = (exponent_terms / totals[..., None]).astype(jnp.bfloat16)
        own_weight = (own_term / totals).astype(jnp.bfloat16)
        mixed = jnp.einsum(
            "bgjk,kgd->bgjd", weights, stored_values, preferred_element_type=jnp.float32
        )
        mixed = (mixed + own_weight.astype(jnp.float32)[..., None] * own_float).astype(jnp.bfloat16)
        matching = (passage_local == index)[:, None, None, None]
        return jnp.where(matching, mixed, result)

    start = jnp.zeros((slot_count, kv_heads, group_size, HD), jnp.bfloat16)
    result = lax.fori_loop(0, pass_local, one_passage, start)
    return result.reshape(slot_count, kv_heads * group_size * HD)


def shards(query, new_kv, kv_store, passage_ids, residual_in, out_weight):
    store_count = lax.axis_size("store")
    local_streams = query.shape[0]
    head_width = query.shape[1]
    kv_width = new_kv.shape[2]
    pass_local = kv_store.shape[1]
    fan_out = min(store_count, 16)
    per_shard = local_streams // fan_out
    slots_total = store_count * per_shard
    stream_passages = passage_ids.reshape(local_streams)
    owner_shard = stream_passages // pass_local
    local_passage = stream_passages - owner_shard * pass_local
    owner_onehot = (owner_shard[:, None] == jnp.arange(store_count)[None, :]).astype(jnp.int32)
    earlier = jnp.cumsum(owner_onehot, axis=0) - owner_onehot
    position = jnp.sum(earlier * owner_onehot, axis=1)
    slot_index = owner_shard * per_shard + position
    slot_match = jnp.arange(slots_total)[:, None] == slot_index[None, :]
    selector = slot_match.astype(jnp.bfloat16)
    gatherer = (slot_index[:, None] == jnp.arange(slots_total)[None, :]).astype(jnp.bfloat16)
    own_pairs = jnp.concatenate([new_kv[0], new_kv[1]], axis=1)
    send_queries = jnp.dot(selector, query, preferred_element_type=jnp.float32).astype(jnp.bfloat16)
    send_pairs = jnp.dot(selector, own_pairs, preferred_element_type=jnp.float32).astype(
        jnp.bfloat16
    )
    send_local = jnp.sum(jnp.where(slot_match, local_passage[None, :], 0), axis=1)
    send_queries = send_queries.reshape(store_count, per_shard, head_width)
    send_pairs = send_pairs.reshape(store_count, per_shard, 2 * kv_width)
    send_local = send_local.reshape(store_count, per_shard)
    recv_queries = lax.all_to_all(send_queries, "store", split_axis=0, concat_axis=0, tiled=True)
    recv_pairs = lax.all_to_all(send_pairs, "store", split_axis=0, concat_axis=0, tiled=True)
    recv_local = lax.all_to_all(send_local, "store", split_axis=0, concat_axis=0, tiled=True)
    sources = recv_queries.shape[0]
    per_source = recv_queries.shape[1]
    results = attend_slots(
        recv_queries.reshape(sources * per_source, head_width),
        recv_pairs.reshape(sources * per_source, 2 * kv_width),
        recv_local.reshape(sources * per_source),
        kv_store,
    )
    results = results.reshape(sources, per_source, head_width)
    returned = lax.all_to_all(results, "store", split_axis=0, concat_axis=0, tiled=True)
    attention = jnp.dot(
        gatherer, returned.reshape(slots_total, head_width), preferred_element_type=jnp.float32
    ).astype(jnp.bfloat16)
    partial_full = jnp.dot(
        attention,
        lax.all_gather(out_weight, "store", axis=1, tiled=True),
        preferred_element_type=jnp.float32,
    )
    projected = lax.psum_scatter(
        partial_full.astype(jnp.bfloat16), "tp", scatter_dimension=1, tiled=True
    ).astype(jnp.float32)
    return (residual_in.astype(jnp.float32) + projected).astype(jnp.bfloat16)


def solution(mesh):
    placed = (
        P("store", "tp"),
        P(None, "store", "tp"),
        P(None, "store", None, "tp"),
        P("store", None),
        P("store", "tp"),
        P("tp", "store"),
    )
    return jax.shard_map(
        shards, mesh=mesh, in_specs=placed, out_specs=P("store", "tp"), check_vma=False
    )
```

profile of v0, /device:TPU:8, one launch (start us, length us, event | category | flops | bytes accessed | tf_op | source)
XLA Modules:
  0.0 264.2 jit_solution(4640889365879576970)
XLA Ops:
  8.6 11.7 %all-to-all-start = ((s32[32,1,5]{2,1,0:T(1,128)}), s32[32,1,5]{2,1,0:T(1,128)S(1)}, u32[]{:S(2)}, u32[]{:S(2)}) async-start(s32[32,1,5]{2,1,0:T(1,128)} %bitcast), calls=%async_computation | async-start | bytes 32768 | tf_op jit(solution)/shard_map/all_to_all | solution.py:86
  21.9 6.9 %all-to-all-done = s32[32,1,5]{2,1,0:T(1,128)S(1)} async-done(((s32[32,1,5]{2,1,0:T(1,128)}), s32[32,1,5]{2,1,0:T(1,128)S(1)}, u32[]{:S(2)}, u32[]{:S(2)}) %all-to-all-start) | async-done | bytes 672 | tf_op jit(solution)/shard_map/all_to_all | solution.py:86
  28.8 4.8 %all-to-all-start.2 = ((bf16[32,5,256]{2,1,0:T(8,128)(2,1)}), bf16[32,5,256]{2,1,0:T(8,128)(2,1)S(1)}, u32[]{:S(2)}, u32[]{:S(2)}) async-start(bf16[32,5,256]{2,1,0:T(8,128)(2,1)} %reshape.233), calls=%async_computation.2 | async-start | bytes 262144 | tf_op jit(solution)/shard_map/all_to_all | solution.py:85
  34.8 7.8 %all-to-all-done.2 = bf16[32,5,256]{2,1,0:T(8,128)(2,1)S(1)} async-done(((bf16[32,5,256]{2,1,0:T(8,128)(2,1)}), bf16[32,5,256]{2,1,0:T(8,128)(2,1)S(1)}, u32[]{:S(2)}, u32[]{:S(2)}) %all-to-all-start.2) | async-done | bytes 81952 | tf_op jit(solution)/shard_map/all_to_all | solution.py:85
  42.6 5.5 %all-to-all-start.1 = ((bf16[32,5,1024]{2,1,0:T(8,128)(2,1)}), bf16[32,5,1024]{2,1,0:T(8,128)(2,1)S(1)}, u32[]{:S(2)}, u32[]{:S(2)}) async-start(bf16[32,5,1024]{2,1,0:T(8,128)(2,1)} %reshape.231), calls=%async_computation.1 | async-start | bytes 1048576 | tf_op jit(solution)/shard_map/all_to_all | solution.py:84
  50.8 12.1 %all-to-all-done.1 = bf16[32,5,1024]{2,1,0:T(8,128)(2,1)S(1)} async-done(((bf16[32,5,1024]{2,1,0:T(8,128)(2,1)}), bf16[32,5,1024]{2,1,0:T(8,128)(2,1)S(1)}, u32[]{:S(2)}, u32[]{:S(2)}) %all-to-all-start.1) | async-done | bytes 327712 | tf_op jit(solution)/shard_map/all_to_all | solution.py:84
  64.1 101.1 %while.14 = (s32[]{:T(128)}, bf16[160,1,8,128]{3,0,2,1:T(8,128)(2,1)S(1)}, s32[160]{0:T(256)}, bf16[2,20,512,128]{3,2,1,0:T(8,128)(2,1)}, bf16[160,1,8,128]{3,0,...) while((s32[]{:T(128)}, ...), condition=%wide.region_6.7_spmd.clone, body=%wide.region_3.6_spmd.clone.sunk | while | flops 342268320 | bytes 9268159 | solution.py:52
  67.2 2.0 fusion.49
  72.2 2.0 fusion.49
  82.3 2.0 fusion.49
  97.5 2.0 fusion.49
  107.6 2.0 fusion.49
  112.6 2.0 fusion.49
  117.7 2.0 fusion.49
  122.7 2.0 fusion.49
  127.8 2.0 fusion.49
  137.9 2.0 fusion.49
  142.9 2.0 fusion.49
  158.1 2.0 fusion.49
  163.1 2.0 fusion.49
  165.7 25.8 %all_to_all.24 = bf16[32,5,1024]{2,1,0:T(8,128)(2,1)S(1)} all-to-all(bf16[32,5,1024]{2,1,0:T(8,128)(2,1)S(1)} %reshape_reshape.7), channel_id=1, replica_groups=mesh['store'=32,'tp'=8] {'store'}, dimensions={0} | all-to-all | bytes 655360 | tf_op jit(solution)/shard_map/all_to_all | solution.py:96
  191.7 20.7 %all-gather.2.cloned.1.call-done = bf16[1024,8192]{1,0:T(8,128)(2,1)} async-done(((bf16[1024,256]{1,0:T(8,128)(2,1)}), bf16[1024,8192]{1,0:T(8,128)(2,1)}) %all-gather.2.cloned.1.call-update) | async-done | bytes 16777232 | tf_op jit(solution)/shard_map/all_gather | solution.py:102
  212.4 10.0 %convolution_convert_fusion = bf16[80,8192]{1,0:T(8,128)(2,1)} fusion(bf16[1024,8192]{1,0:T(8,128)(2,1)} %all-gather.2.cloned.1.call-done, bf16[160,1024]{1,0:T(8,128)(2,1)S(1)} %reshape.235, s32[80]{0:T(128)S(1)} %copy-done.4), kind=kOutput, calls=%fused_computation.26 | convolution fusion | flops 1369141760 | bytes 18415936 | tf_op jit(solution)/shard_map/dot_general | solution.py:100
  222.4 33.3 %reduce-scatter.2.cloned.1.call-done = bf16[80,1024]{1,0:T(8,128)(2,1)} async-done(((bf16[80,8192]{1,0:T(8,128)(2,1)}), bf16[80,1024]{1,0:T(8,128)(2,1)}) %reduce-scatter.2.cloned.1.call-update) | async-done | bytes 163856 | tf_op jit(solution)/shard_map/reduce_scatter | solution.py:105
  (188 shorter events, 84.9 us)
Async XLA Ops:
  6.5 27.1 %copy-start = (bf16[80,1024]{1,0:T(8,128)(2,1)S(1)}, bf16[80,1024]{1,0:T(8,128)(2,1)}, u32[]{:S(2)}) copy-start(bf16[80,1024]{1,0:T(8,128)(2,1)} %param.8) | copy-start | bytes 491524
  7.7 41.1 %copy-start.3 = (s32[80]{0:T(128)}, s32[80]{0:T(128)S(1)}, u32[]{:S(2)}) copy-start(s32[80]{0:T(128)S(1)} %multiply_add_fusion) | copy-start | bytes 964
  8.6 20.2 %all-to-all-start = ((s32[32,1,5]{2,1,0:T(1,128)}), s32[32,1,5]{2,1,0:T(1,128)S(1)}, u32[]{:S(2)}, u32[]{:S(2)}) async-start(s32[32,1,5]{2,1,0:T(1,128)} %bitcast), calls=%async_computation | async-start | bytes 32768 | tf_op jit(solution)/shard_map/all_to_all | solution.py:86
  28.8 13.8 %all-to-all-start.2 = ((bf16[32,5,256]{2,1,0:T(8,128)(2,1)}), bf16[32,5,256]{2,1,0:T(8,128)(2,1)S(1)}, u32[]{:S(2)}, u32[]{:S(2)}) async-start(bf16[32,5,256]{2,1,0:T(8,128)(2,1)} %reshape.233), calls=%async_computation.2 | async-start | bytes 262144 | tf_op jit(solution)/shard_map/all_to_all | solution.py:85
  42.6 20.3 %all-to-all-start.1 = ((bf16[32,5,1024]{2,1,0:T(8,128)(2,1)}), bf16[32,5,1024]{2,1,0:T(8,128)(2,1)S(1)}, u32[]{:S(2)}, u32[]{:S(2)}) async-start(bf16[32,5,1024]{2,1,0:T(8,128)(2,1)} %reshape.231), calls=%async_computation.1 | async-start | bytes 1048576 | tf_op jit(solution)/shard_map/all_to_all | solution.py:84
  48.1 164.3 %all-gather.2.cloned.1.call-start = ((), (), s32[]{:S(2)}) async-start(), calls=%async_computation.5 | async-start | bytes 17301504 | tf_op jit(solution)/shard_map/all_gather | solution.py:102
  48.8 207.0 %reduce-scatter.2.cloned.1.call-start = ((), (), s32[]{:S(2)}) async-start(), calls=%async_computation.6 | async-start | bytes 1474560 | tf_op jit(solution)/shard_map/reduce_scatter | solution.py:105
  64.1 2.5 copy-start.2
  74.2 2.5 copy-start.2
  79.3 2.5 copy-start.2
  84.4 2.5 copy-start.2
  94.4 2.5 copy-start.2
  99.5 2.5 copy-start.2
  109.6 2.5 copy-start.2
  114.7 2.5 copy-start.2
  119.7 2.5 copy-start.2
  129.8 2.5 copy-start.2
  134.9 2.5 copy-start.2
  139.9 2.5 copy-start.2
  145.0 2.5 copy-start.2
  155.1 2.5 copy-start.2
  160.1 2.5 copy-start.2
  165.2 47.2 %copy-start.4 = (s32[80]{0:T(128)S(1)}, s32[80]{0:T(128)}, u32[]{:S(2)}) copy-start(s32[80]{0:T(128)} %copy-done.3) | copy-start | bytes 964
  191.7 64.1 %copy-start.1 = (bf16[80,1024]{1,0:T(8,128)(2,1)S(1)}, bf16[80,1024]{1,0:T(8,128)(2,1)}, u32[]{:S(2)}) copy-start(bf16[80,1024]{1,0:T(8,128)(2,1)} %param.12) | copy-start | bytes 491524
  (5 other events, 12.3 us)
Sparse Core Ops, SparseCore 0:
  51.4 160.9 all-gather.1
  222.5 33.1 reduce-scatter.1
where the time goes:
time: 265 us; the launch traced here: 264 us
  waiting for transfers between devices  81.5 us (31%)
  matrix products  81.3 us (31%)
  other arithmetic  32.2 us (12%)
  blocking collectives  25.8 us (10%)
  starting transfers between devices  22 us (8%)
  between operations  13.6 us (5%)
  local copies, waits for them, and re-layouts  6.82 us (3%)
    dot_general x20, matrix products, one_passage(): jnp.einsum('bgjk,kgd->bgjd', weights, stored_values, preferred_element_ty...  40.2 us
    reduce_scatter x1, waiting for transfers between devices, shards(): lax.psum_scatter(partial_full.astype(jnp.bfloat16), 'tp', scatter_dimensi...  33.3 us
    dot_general x20, matrix products, one_passage(): jnp.einsum('bgjd,kgd->bgjk', query_heads, stored_keys, preferred_element_...  30.4 us
    all_to_all x1, blocking collectives, shards(): lax.all_to_all(results, 'store', split_axis=0, concat_axis=0, tiled=True)  25.8 us
    all_gather x1, waiting for transfers between devices, shards(): lax.all_gather(out_weight, 'store', axis=1, tiled=True)  20.7 us
    reduce_sum x20, other arithmetic, one_passage(): totals = jnp.sum(exponent_terms, axis=-1) + own_term  18.1 us
    all_to_all x1, waiting for transfers between devices, shards(): lax.all_to_all(send_queries, 'store', split_axis=0, concat_axis=0, tiled=...  12.1 us
    all_to_all x1, starting transfers between devices, shards(): lax.all_to_all(send_local, 'store', split_axis=0, concat_axis=0, tiled=True)  11.7 us
  transfers between devices with their start and end apart: 5, of which 5 were waited for; matrix products, arithmetic and copies ran while one was open for 40% of the time, Pallas kernels for 0%

commit v1 on v0

--- a/solution.py
+++ b/solution.py
@@ -99,7 +99,9 @@
     ).astype(jnp.bfloat16)
     partial_full = jnp.dot(
         attention,
-        lax.all_gather(out_weight, "store", axis=1, tiled=True),
+        jnp.concatenate(
+            lax.all_to_all(jnp.stack([out_weight] * lax.axis_size("store")), "store", 0, 0), axis=1
+        ),
         preferred_element_type=jnp.float32,
     )
     projected = lax.psum_scatter(

time: 265 us -> 633 us (2.39)
  waiting for transfers between devices: 81.5 us -> 454 us
  blocking collectives: 25.8 us -> 0 us
  starting transfers between devices: 22 us -> 34.2 us
  local copies, waits for them, and re-layouts: 6.82 us -> 13.8 us
    all_to_all x0 -> x2, waiting for transfers between devices: none -> 376 us  [the longest x1 362 us: shards(): lax.all_to_all(jnp.stack([out_weight] * lax.axis_size('store')), 'store',...]
    all_to_all x1 -> x0, blocking collectives: 25.8 us -> none  [shards(): lax.all_to_all(results, 'store', split_axis=0, concat_axis=0, tiled=True)]
    all_gather x1 -> x0, waiting for transfers between devices: 20.7 us -> none  [shards(): lax.all_gather(out_weight, 'store', axis=1, tiled=True)]
    reduce_scatter x1, waiting for transfers between devices: 33.3 us -> 51.5 us  [shards(): lax.psum_scatter(partial_full.astype(jnp.bfloat16), 'tp', scatter_dimensi...]
    all_to_all x0 -> x2, starting transfers between devices: none -> 12 us  [the longest x1 6.42 us: shards(): lax.all_to_all(jnp.stack([out_weight] * lax.axis_size('store')), 'store',...]
  transfers between devices with their start and end apart: 5 -> 6, of which waited for: 5 -> 6; matrix products, arithmetic and copies ran while one was open for 40% -> 1% of each run, Pallas kernels for 0% -> 0%
where the time goes in v1:
time: 633 us; the launch traced here: 632 us
  waiting for transfers between devices  454 us (72%)
  matrix products  83.3 us (13%)
  starting transfers between devices  34.2 us (5%)
  other arithmetic  31.8 us (5%)
  local copies, waits for them, and re-layouts  13.8 us (2%)
  between operations  13.6 us (2%)
    all_to_all x1, waiting for transfers between devices, shards(): lax.all_to_all(jnp.stack([out_weight] * lax.axis_size('store')), 'store',...  362 us
    reduce_scatter x1, waiting for transfers between devices, shards(): lax.psum_scatter(partial_full.astype(jnp.bfloat16), 'tp', scatter_dimensi...  51.5 us
    dot_general x20, matrix products, one_passage(): jnp.einsum('bgjk,kgd->bgjd', weights, stored_values, preferred_element_ty...  40.1 us
    dot_general x20, matrix products, one_passage(): jnp.einsum('bgjd,kgd->bgjk', query_heads, stored_keys, preferred_element_...  30.3 us
    reduce_sum x20, other arithmetic, one_passage(): totals = jnp.sum(exponent_terms, axis=-1) + own_term  18.1 us
    all_to_all x1, waiting for transfers between devices, shards(): lax.all_to_all(results, 'store', split_axis=0, concat_axis=0, tiled=True)  13.5 us
  transfers between devices with their start and end apart: 6, of which 6 were waited for; matrix products, arithmetic and copies ran while one was open for 1% of the time, Pallas kernels for 0%

profile of v1, /device:TPU:8, one launch (start us, length us, event | category | flops | bytes accessed | tf_op | source)
XLA Modules:
  0.0 632.2 jit_solution(16618478461253294991)
XLA Ops:
  8.6 11.7 %all-to-all-start = ((s32[32,1,5]{2,1,0:T(1,128)}), s32[32,1,5]{2,1,0:T(1,128)S(1)}, u32[]{:S(2)}, u32[]{:S(2)}) async-start(s32[32,1,5]{2,1,0:T(1,128)} %bitcast), calls=%async_computation | async-start | bytes 32768 | tf_op jit(solution)/shard_map/all_to_all | solution.py:86
  21.9 6.9 %all-to-all-done = s32[32,1,5]{2,1,0:T(1,128)S(1)} async-done(((s32[32,1,5]{2,1,0:T(1,128)}), s32[32,1,5]{2,1,0:T(1,128)S(1)}, u32[]{:S(2)}, u32[]{:S(2)}) %all-to-all-start) | async-done | bytes 672 | tf_op jit(solution)/shard_map/all_to_all | solution.py:86
  28.8 5.0 all-to-all-start.2
  35.0 7.8 %all-to-all-done.2 = bf16[32,5,256]{2,1,0:T(8,128)(2,1)S(1)} async-done(((bf16[32,5,256]{2,1,0:T(8,128)(2,1)}), bf16[32,5,256]{2,1,0:T(8,128)(2,1)S(1)}, u32[]{:S(2)}, u32[]{:S(2)}) %all-to-all-start.2) | async-done | bytes 81952 | tf_op jit(solution)/shard_map/all_to_all | solution.py:85
  42.7 5.5 all-to-all-start.1
  50.3 12.4 %all-to-all-done.1 = bf16[32,5,1024]{2,1,0:T(8,128)(2,1)S(1)} async-done(((bf16[32,5,1024]{2,1,0:T(8,128)(2,1)}), bf16[32,5,1024]{2,1,0:T(8,128)(2,1)S(1)}, u32[]{:S(2)}, u32[]{:S(2)}) %all-to-all-start.1) | async-done | bytes 327712 | tf_op jit(solution)/shard_map/all_to_all | solution.py:84
  63.9 100.5 %while.14 = (s32[]{:T(128)}, bf16[160,1,8,128]{3,0,2,1:T(8,128)(2,1)S(1)}, s32[160]{0:T(256)}, bf16[2,20,512,128]{3,2,1,0:T(8,128)(2,1)}, bf16[160,1,8,128]{3,0,...) while((s32[]{:T(128)}, ...), condition=%wide.region_6.7_spmd.clone, body=%wide.region_3.6_spmd.clone.sunk | while | flops 342268320 | bytes 9267151 | solution.py:52
  87.0 2.0 fusion.49
  92.1 2.0 fusion.49
  97.1 2.0 fusion.49
  102.1 2.0 fusion.49
  107.2 2.0 fusion.49
  112.2 2.0 fusion.49
  117.2 2.0 fusion.49
  122.2 2.0 fusion.49
  127.3 2.0 fusion.49
  147.4 2.0 fusion.49
  165.8 5.6 all-to-all-start.3
  171.6 13.5 %all-to-all-done.3 = bf16[32,5,1024]{2,1,0:T(8,128)(2,1)S(1)} async-done(((bf16[32,5,1024]{2,1,0:T(8,128)(2,1)}), bf16[32,5,1024]{2,1,0:T(8,128)(2,1)S(1)}, u32[]{:S(2)}, u32[]{:S(2)}) %all-to-all-start.3) | async-done | bytes 327712 | tf_op jit(solution)/shard_map/all_to_all | solution.py:96
  185.2 6.0 stack.2
  191.1 6.4 %all-to-all-start.4 = ((bf16[32,1024,256]{1,2,0:T(8,128)(2,1)}), bf16[32,1024,256]{1,2,0:T(8,128)(2,1)}, u32[]{:S(2)}, u32[]{:S(2)}) async-start(bf16[32,1024,256]{1,2,0:T(8,128)(2,1)} %stack.2), calls=%async_computation.4 | async-start | bytes 33554432 | tf_op jit(solution)/shard_map/all_to_all | solution.py:103
  197.7 362.2 %all-to-all-done.4 = bf16[32,1024,256]{1,2,0:T(8,128)(2,1)} async-done(((bf16[32,1024,256]{1,2,0:T(8,128)(2,1)}), bf16[32,1024,256]{1,2,0:T(8,128)(2,1)}, u32[]{:S(2)}, u32[]{:S(2)}) %all-to-all-start.4) | async-done | bytes 16777248 | tf_op jit(solution)/shard_map/all_to_all | solution.py:103
  560.0 12.2 %convolution_convert_fusion = bf16[80,8192]{1,0:T(8,128)(2,1)} fusion(bf16[1024,8192]{0,1:T(8,128)(2,1)} %bitcast.8, bf16[160,1024]{1,0:T(8,128)(2,1)S(1)} %reshape.243, s32[80]{0:T(128)S(1)} %copy-done.5), kind=kOutput, calls=%fused_computation.26 | convolution fusion | flops 1369141760 | bytes 18415936 | tf_op jit(solution)/shard_map/dot_general | solution.py:100
  572.2 51.5 %reduce-scatter.2.cloned.1.call-done = bf16[80,1024]{1,0:T(8,128)(2,1)} async-done(((bf16[80,8192]{1,0:T(8,128)(2,1)}), bf16[80,1024]{1,0:T(8,128)(2,1)}) %reduce-scatter.2.cloned.1.call-update) | async-done | bytes 163856 | tf_op jit(solution)/shard_map/reduce_scatter | solution.py:107
  (192 shorter events, 90.7 us)
Async XLA Ops:
  6.5 27.3 %copy-start = (bf16[80,1024]{1,0:T(8,128)(2,1)S(1)}, bf16[80,1024]{1,0:T(8,128)(2,1)}, u32[]{:S(2)}) copy-start(bf16[80,1024]{1,0:T(8,128)(2,1)} %param.8) | copy-start | bytes 491524
  7.7 40.6 %copy-start.4 = (s32[80]{0:T(128)}, s32[80]{0:T(128)S(1)}, u32[]{:S(2)}) copy-start(s32[80]{0:T(128)S(1)} %multiply_add_fusion) | copy-start | bytes 964
  8.6 20.2 %all-to-all-start = ((s32[32,1,5]{2,1,0:T(1,128)}), s32[32,1,5]{2,1,0:T(1,128)S(1)}, u32[]{:S(2)}, u32[]{:S(2)}) async-start(s32[32,1,5]{2,1,0:T(1,128)} %bitcast), calls=%async_computation | async-start | bytes 32768 | tf_op jit(solution)/shard_map/all_to_all | solution.py:86
  28.8 13.9 %all-to-all-start.2 = ((bf16[32,5,256]{2,1,0:T(8,128)(2,1)}), bf16[32,5,256]{2,1,0:T(8,128)(2,1)S(1)}, u32[]{:S(2)}, u32[]{:S(2)}) async-start(bf16[32,5,256]{2,1,0:T(8,128)(2,1)} %reshape.241), calls=%async_computation.2 | async-start | bytes 262144 | tf_op jit(solution)/shard_map/all_to_all | solution.py:85
  42.7 19.9 %all-to-all-start.1 = ((bf16[32,5,1024]{2,1,0:T(8,128)(2,1)}), bf16[32,5,1024]{2,1,0:T(8,128)(2,1)S(1)}, u32[]{:S(2)}, u32[]{:S(2)}) async-start(bf16[32,5,1024]{2,1,0:T(8,128)(2,1)} %reshape.239), calls=%async_computation.1 | async-start | bytes 1048576 | tf_op jit(solution)/shard_map/all_to_all | solution.py:84
  63.9 2.5 copy-start.3
  79.0 2.5 copy-start.3
  84.0 2.5 copy-start.3
  89.1 2.5 copy-start.3
  94.1 2.5 copy-start.3
  99.1 2.5 copy-start.3
  104.2 2.5 copy-start.3
  109.2 2.5 copy-start.3
  114.2 2.5 copy-start.3
  119.2 2.5 copy-start.3
  124.3 2.5 copy-start.3
  129.3 2.5 copy-start.3
  134.3 2.5 copy-start.3
  164.5 6.9 %copy-start.1 = (bf16[1024,256]{1,0:T(8,128)(2,1)S(1)}, bf16[1024,256]{1,0:T(8,128)(2,1)}, u32[]{:S(2)}) copy-start(bf16[1024,256]{1,0:T(8,128)(2,1)} %param.13) | copy-start | bytes 1572868
  165.8 19.4 %all-to-all-start.3 = ((bf16[32,5,1024]{2,1,0:T(8,128)(2,1)}), bf16[32,5,1024]{2,1,0:T(8,128)(2,1)S(1)}, u32[]{:S(2)}, u32[]{:S(2)}) async-start(bf16[32,5,1024]{2,1,0:T(8,128)(2,1)} %reshape_reshape.7), calls=%async_computation.3 | async-start | bytes 1048576 | tf_op jit(solution)/shard_map/all_to_all | solution.py:96
  191.1 368.9 %copy-start.5 = (s32[80]{0:T(128)S(1)}, s32[80]{0:T(128)}, u32[]{:S(2)}) copy-start(s32[80]{0:T(128)} %copy-done.4) | copy-start | bytes 964
  191.1 368.9 %all-to-all-start.4 = ((bf16[32,1024,256]{1,2,0:T(8,128)(2,1)}), bf16[32,1024,256]{1,2,0:T(8,128)(2,1)}, u32[]{:S(2)}, u32[]{:S(2)}) async-start(bf16[32,1024,256]{1,2,0:T(8,128)(2,1)} %stack.2), calls=%async_computation.4 | async-start | bytes 33554432 | tf_op jit(solution)/shard_map/all_to_all | solution.py:103
  197.5 426.1 %reduce-scatter.2.cloned.1.call-start = ((), (), s32[]{:S(2)}) async-start(), calls=%async_computation.6 | async-start | bytes 1474560 | tf_op jit(solution)/shard_map/reduce_scatter | solution.py:107
  560.0 63.7 %copy-start.2 = (bf16[80,1024]{1,0:T(8,128)(2,1)S(1)}, bf16[80,1024]{1,0:T(8,128)(2,1)}, u32[]{:S(2)}) copy-start(bf16[80,1024]{1,0:T(8,128)(2,1)} %param.12) | copy-start | bytes 491524
  (7 other events, 17.2 us)
Sparse Core Ops, SparseCore 0:
  572.3 51.2 reduce-scatter.1
